TPU v7x, 128 devices: a whole 4x4x4 slice. The times are simulated.
128 devices in a mesh: fsdp: 16 (over z, x_lo, core), tp: 8 (over y, x_hi).
Axes of the slice: x: 4 (x_hi: 2, x_lo: 2; x = x_hi * 2 + x_lo), y: 4, z: 4, core: 2. Of those that a mesh axis runs over, the one named last changes fastest.
Arguments:
- hidden_in: bfloat16 [2048, 4, 8192], P('fsdp'), may hold values from -6 to 6
- lengths: int32 [2048], P('fsdp'), may hold values from 1 to 128, as said below
- key_cache: bfloat16 [2048, 128, 1024], P('fsdp', None, 'tp'), may hold values from -400 to 400
- value_cache: bfloat16 [2048, 128, 1024], P('fsdp', None, 'tp'), may hold values from -6 to 6
- query_weight: bfloat16 [8192, 4096], P('fsdp'), may hold values from -0.0625 to 0.0625
- key_weight: bfloat16 [8192, 1024], P('fsdp'), may hold values from -0.0625 to 0.0625
- value_weight: bfloat16 [8192, 1024], P('fsdp'), may hold values from -0.0625 to 0.0625
- out_weight: bfloat16 [4096, 8192], P(None, 'fsdp'), may hold values from -0.5 to 0.5
Outputs:
- attn_out: bfloat16 [2048, 4, 8192], P('fsdp')
Inputs may be any that keep to these rules, and one draw needn't show every extreme that they name: `lengths`: some row fills all 128 slots; slots at or beyond a row's length hold stale data.
All inputs are finite; a program needn't handle non-finite values.
Results may differ from a plain program's by a relative error of at most 0.012.
Values may be sent and summed in bfloat16 or wider, within the bound.
A program may use at most 192 MiB of HBM per device.

v0:
```python
import math

import jax
import jax.numpy as jnp
from jax import lax
from jax.sharding import PartitionSpec as P

HQ = 32
KVH = 8
HD = 128


rope_base = 1000000.0
epsilon = 1e-06
masked = -1e30


def rotate(values, positions):
    middle = values.shape[-1] // 2
    frequency = rope_base ** (-(jnp.arange(middle, dtype=jnp.float32) * 2.0) / values.shape[-1])
    angles = positions.astype(jnp.float32)[..., None] * frequency
    cosine = jnp.cos(angles)
    sine_part = jnp.sin(angles)
    former = values[..., :middle]
    latter = values[..., middle:]
    return jnp.concatenate(
        [former * cosine - latter * sine_part, latter * cosine + former * sine_part], axis=-1
    )


def attend(queries, key_cache, value_cache, fresh_keys, fresh_values, lengths):
    row_count, step_count, head_groups, group_size, head_size = queries.shape
    slot_count = key_cache.shape[1]
    cached_keys = key_cache.reshape(row_count, slot_count, head_groups, head_size)
    cached_values = value_cache.reshape(row_count, slot_count, head_groups, head_size)
    scaling = 1.0 / math.sqrt(head_size)
    older_scores = (
        jnp.einsum("rsgqd,rlgd->rsgql", queries, cached_keys, preferred_element_type=jnp.float32)
        * scaling
    )
    recent = (
        jnp.einsum("rsgqd,rtgd->rsgqt", queries, fresh_keys, preferred_element_type=jnp.float32)
        * scaling
    )
    live_slots = lax.broadcasted_iota(jnp.int32, (row_count, slot_count), 1) < lengths[:, None]
    older_scores = jnp.where(live_slots[:, None, None, None, :], older_scores, masked)
    causal = lax.broadcasted_iota(jnp.int32, (step_count, step_count), 1) <= lax.broadcasted_iota(
        jnp.int32, (step_count, step_count), 0
    )
    recent = jnp.where(causal[None, :, None, None, :], recent, masked)
    highest = jnp.maximum(jnp.max(older_scores, axis=-1), jnp.max(recent, axis=-1))[..., None]
    older_exp = jnp.exp(older_scores - highest)
    recent_exp = jnp.exp(recent - highest)
    totals = jnp.sum(older_exp, axis=-1, keepdims=True) + jnp.sum(
        recent_exp, axis=-1, keepdims=True
    )
    older_prob = (older_exp / totals).astype(jnp.bfloat16)
    recent_prob = (recent_exp / totals).astype(jnp.bfloat16)
    mixture = jnp.einsum(
        "rsgql,rlgd->rsgqd", older_prob, cached_values, preferred_element_type=jnp.float32
    )
    mixture = mixture + jnp.einsum(
        "rsgqt,rtgd->rsgqd", recent_prob, fresh_values, preferred_element_type=jnp.float32
    )
    return mixture.astype(jnp.bfloat16)


def head_total(partial_blocks):
    return lax.psum(partial_blocks, "tp").astype(jnp.bfloat16)


def body(
    hidden_in, lengths, key_cache, value_cache, query_weight, key_weight, value_weight, out_weight
):
    row_count, step_count, model_width = hidden_in.shape
    token_count = row_count * step_count
    tp_rank = lax.axis_index("tp")
    tp_count = lax.axis_size("tp")
    kv_width = key_cache.shape[2]
    group_size = HQ // KVH
    head_groups = kv_width // HD
    query_width = kv_width * group_size
    flat_rows = hidden_in.astype(jnp.float32).reshape(token_count, model_width)
    normed = (
        flat_rows * lax.rsqrt(jnp.mean(flat_rows * flat_rows, axis=1, keepdims=True) + epsilon)
    ).astype(jnp.bfloat16)
    query_cols = lax.dynamic_slice_in_dim(query_weight, tp_rank * query_width, query_width, 1)
    key_cols = lax.dynamic_slice_in_dim(key_weight, tp_rank * kv_width, kv_width, 1)
    value_cols = lax.dynamic_slice_in_dim(value_weight, tp_rank * kv_width, kv_width, 1)
    queries = jnp.dot(
        normed,
        lax.all_gather(query_cols, "fsdp", axis=0, tiled=True),
        preferred_element_type=jnp.float32,
    )
    keys_raw = jnp.dot(
        normed,
        lax.all_gather(key_cols, "fsdp", axis=0, tiled=True),
        preferred_element_type=jnp.float32,
    )
    values_raw = jnp.dot(
        normed,
        lax.all_gather(value_cols, "fsdp", axis=0, tiled=True),
        preferred_element_type=jnp.float32,
    )
    offsets = lax.broadcasted_iota(jnp.int32, (row_count, step_count), 1)
    positions = lengths[:, None] + offsets
    rotated_queries = rotate(
        queries.reshape(row_count, step_count, head_groups, group_size, HD),
        positions[:, :, None, None],
    ).astype(jnp.bfloat16)
    rotated_keys = rotate(
        keys_raw.reshape(row_count, step_count, head_groups, HD), positions[:, :, None]
    ).astype(jnp.bfloat16)
    new_values = values_raw.reshape(row_count, step_count, head_groups, HD).astype(jnp.bfloat16)
    context = attend(
        rotated_queries, key_cache, value_cache, rotated_keys, new_values, lengths
    ).reshape(token_count, query_width)
    out_rows = lax.dynamic_slice_in_dim(out_weight, tp_rank * query_width, query_width, 0)
    partial_terms = jnp.dot(
        context,
        lax.all_gather(out_rows, "fsdp", axis=1, tiled=True),
        preferred_element_type=jnp.float32,
    )
    blocks = partial_terms.reshape(token_count, tp_count, 1, model_width // tp_count)
    result = head_total(blocks).reshape(token_count, model_width)
    return result.reshape(row_count, step_count, model_width)


def solution(mesh):
    return jax.shard_map(
        body,
        mesh=mesh,
        in_specs=(
            P("fsdp", None, None),
            P("fsdp"),
            P("fsdp", None, "tp"),
            P("fsdp", None, "tp"),
            P("fsdp", None),
            P("fsdp", None),
            P("fsdp", None),
            P(None, "fsdp"),
        ),
        out_specs=P("fsdp", None, None),
        check_vma=False,
    )
```

profile of v0, /device:TPU:0, one launch (start us, length us, event | category | flops | bytes accessed | tf_op | source)
XLA Modules:
  0.0 931.5 jit_solution(5404717578202475878)
XLA Ops:
  6.5 0.0 all-gather.7.cloned.1.call-start
  6.5 1.2 copy-done
  7.8 0.8 copy.67
  8.6 0.0 all-gather.7.cloned.1.call-update
  8.6 0.0 all-gather.9.cloned.1.call-start
  8.7 1.6 constant_dynamic-slice_fusion.1
  10.2 0.0 all-gather.9.cloned.1.call-update
  10.2 0.0 all-gather.5.cloned.1.call-start
  10.3 1.9 constant_dynamic-slice_fusion.3
  12.2 0.0 all-gather.5.cloned.1.call-update
  12.2 0.0 all-gather.11.cloned.1.call-start
  12.3 1.9 constant_dynamic-slice_fusion
  14.2 0.0 all-gather.11.cloned.1.call-update
  14.2 0.7 add_convert_fusion.1
  14.9 0.7 iota_compare_fusion
  15.6 7.8 fusion
  23.4 0.5 multiply_cosine_fusion.1
  24.0 0.0 slice-start.1
  24.0 10.2 %fusion.1 = bf16[128,4,8192]{2,1,0:T(4,128)(2,1)} fusion(bf16[128,4,8192]{2,1,0:T(4,128)(2,1)} %param.8, f32[128,4]{1,0:T(8,128)S(1)} %add_rsqrt_fusion), kind=kLoop, calls=%fused_computation.3 | loop fusion | flops 12582912 | bytes 16779264 | tf_op jit(solution)/shard_map/convert_element_type | solution.py:86
  34.2 0.0 slice-done
  34.2 6.3 fusion.85
  40.5 5.0 all-gather.7.cloned.1.call-done
  45.6 13.0 %fusion.36 = f32[128,4,1,128]{0,3,1,2:T(8,128)S(1)} fusion(bf16[8192,128]{0,1:T(8,128)(2,1)} %all-gather.7.cloned.1.call-done, bf16[128,4,8192]{2,1,0:T(4,128)(2,1)} %fusion.1), kind=kOutput, calls=%fused_computation.26 | convolution fusion | flops 1073741824 | bytes 10747904 | tf_op jit(solution)/shard_map/dot_general | solution.py:95
  58.6 0.6 fusion.76
  59.2 0.1 copy.57
  59.3 22.1 %all-gather.9.cloned.1.call-done = bf16[8192,128]{1,0:T(8,128)(2,1)} async-done(((bf16[512,128]{1,0:T(8,128)(2,1)}), bf16[8192,128]{1,0:T(8,128)(2,1)}) %all-gather.9.cloned.1.call-update) | async-done | bytes 2097168 | tf_op jit(solution)/shard_map/all_gather | solution.py:102
  81.4 13.0 %fusion.46 = bf16[128,4,128,1]{2,0,1,3:T(8,128)(2,1)S(1)} fusion(bf16[8192,128]{1,0:T(8,128)(2,1)} %all-gather.9.cloned.1.call-done, bf16[128,4,8192]{2,1,0:T(4,128)(2,1)} %fusion.1), kind=kOutput, calls=%fused_computation.28 | convolution fusion | flops 1073807360 | bytes 10616832 | tf_op jit(solution)/shard_map/dot_general | solution.py:100
  94.5 40.6 %all-gather.5.cloned.1.call-done = bf16[8192,512]{1,0:T(8,128)(2,1)} async-done(((bf16[512,512]{1,0:T(8,128)(2,1)}), bf16[8192,512]{1,0:T(8,128)(2,1)}) %all-gather.5.cloned.1.call-update) | async-done | bytes 8388624 | tf_op jit(solution)/shard_map/all_gather | solution.py:92
  135.1 11.9 %copy.43 = bf16[512,8192]{1,0:T(8,128)(2,1)} copy(bf16[512,8192]{0,1:T(8,128)(2,1)} %bitcast.115) | data formatting | bytes 16777216 | tf_op jit(solution)/shard_map/dot_general | solution.py:90
  147.1 42.8 %all-gather.11.cloned.1.call-done = bf16[512,8192]{1,0:T(8,128)(2,1)} async-done(((bf16[512,512]{1,0:T(8,128)(2,1)}), bf16[512,8192]{1,0:T(8,128)(2,1)}) %all-gather.11.cloned.1.call-update) | async-done | bytes 8388624 | tf_op jit(solution)/shard_map/all_gather | solution.py:121
  189.8 12.0 %copy.53 = bf16[8192,512]{1,0:T(8,128)(2,1)} copy(bf16[8192,512]{0,1:T(8,128)(2,1)} %bitcast.116) | data formatting | bytes 16777216 | tf_op jit(solution)/shard_map/dot_general | solution.py:119
  201.8 19.5 %fusion.14 = f32[128,4,1,4,128]{0,4,3,1,2:T(8,128)S(1)} fusion(bf16[4,128,8192,1]{2,1,0,3:T(8,128)(2,1)} %bitcast.117, bf16[128,4,8192,1]{2,1,0,3:T(4,128)(2,1)} %fusion.85), kind=kOutput, calls=%fused_computation.17 | convolution fusion | flops 4294967296 | bytes 17825792 | tf_op jit(solution)/shard_map/dot_general | solution.py:90
  221.3 0.1 fusion.64
  221.5 0.4 copy.45
  221.9 4.7 fusion.78
  226.7 0.0 copy-start.2
  226.7 4.8 fusion.77
  231.5 0.1 max.9
  231.6 1.0 fusion.59
  232.6 1.4 fusion.58
  233.9 0.1 add.66
  234.0 0.9 fusion.60
  234.9 2.0 fusion.33
  236.9 0.2 reshape.275
  237.1 11.5 %convolution_bitcast_fusion = f32[512,8,1,1024]{3,0,1,2:T(8,128)} fusion(bf16[512,512,1]{1,0,2:T(8,128)(2,1)S(1)} %reshape.275, bf16[8,1024,512]{2,1,0:T(8,128)(2,1)} %bitcast.114), kind=kOutput, calls=%fused_computation.4 | convolution fusion | flops 4294967296 | bytes 25690112 | tf_op jit(solution)/shard_map/dot_general | solution.py:119
  248.6 650.0 %all-reduce.1 = bf16[512,8,1,1024]{3,0,1,2:T(8,128)(2,1)} all-reduce(f32[512,8,1,1024]{3,0,1,2:T(8,128)} %convolution_bitcast_fusion), channel_id=1, replica_groups=mesh['fsdp'=16,'tp'=8] {'tp'}, use_global_device_ids=true, to_apply=%region_5.6 | all-reduce | flops 4194304 | bytes 25165824 | tf_op jit(solution)/shard_map/psum | solution.py:69
  898.6 11.4 %copy.54 = bf16[512,8,1,1024]{3,1,0,2:T(8,128)(2,1)} copy(bf16[512,8,1,1024]{3,0,1,2:T(8,128)(2,1)} %all-reduce.1) | data formatting | bytes 16777216 | tf_op jit(solution)/shard_map/convert_element_type | solution.py:69
  910.0 14.5 %reshape_reshape.3 = bf16[128,4,8192]{2,1,0:T(4,128)(2,1)} reshape(bf16[512,8,1,1024]{3,1,0,2:T(8,128)(2,1)} %copy.54) | data formatting | bytes 16777216 | tf_op jit(solution)/shard_map/reshape;reshape | solution.py:126
  (13 shorter events, 0.1 us)
Async XLA Ops:
  6.5 1.2 copy-start
  6.5 39.0 %all-gather.7.cloned.1.call-start = ((), (), s32[]{:S(2)}) async-start(), calls=%async_computation.1 | async-start | bytes 2228224 | tf_op jit(solution)/shard_map/all_gather | solution.py:97
  8.6 72.8 %all-gather.9.cloned.1.call-start = ((), (), s32[]{:S(2)}) async-start(), calls=%async_computation.2 | async-start | bytes 2228224 | tf_op jit(solution)/shard_map/all_gather | solution.py:102
  10.2 124.9 %all-gather.5.cloned.1.call-start = ((), (), s32[]{:S(2)}) async-start(), calls=%async_computation | async-start | bytes 8912896 | tf_op jit(solution)/shard_map/all_gather | solution.py:92
  12.2 177.6 %all-gather.11.cloned.1.call-start = ((), (), s32[]{:S(2)}) async-start(), calls=%async_computation.3 | async-start | bytes 8912896 | tf_op jit(solution)/shard_map/all_gather | solution.py:121
  23.4 10.8 %slice-start = ((s8[8388608]{0:T(1024)(128)(4,1)}), s8[4194304]{0:T(1024)(128)(4,1)S(1)}, s32[]{:S(2)}) async-start(s8[8388608]{0:T(1024)(128)(4,1)} %bitcast.112), calls=%async_computation.4 | async-start | bytes 8388608
  24.0 10.2 %slice-start.1 = ((s8[8388608]{0:T(1024)(128)(4,1)}), s8[4194304]{0:T(1024)(128)(4,1)S(1)}, s32[]{:S(2)}) async-start(s8[8388608]{0:T(1024)(128)(4,1)} %bitcast.112), calls=%async_computation.5 | async-start | bytes 8388608
  226.7 8.2 copy-start.2
  898.6 25.9 %copy-start.1 = (bf16[512,1024]{1,0:T(8,128)(2,1)S(1)}, bf16[512,1024]{1,0:T(8,128)(2,1)}, u32[]{:S(2)}) copy-start(bf16[512,1024]{1,0:T(8,128)(2,1)} %param.13) | copy-start | bytes 3145732
Sparse Core Ops, SparseCore 0:
  9.0 36.4 all-gather.6
  47.3 34.1 all-gather.8
  83.2 51.9 all-gather.4
  136.7 53.1 all-gather.10
where the time goes:
time: 938 us; the launch traced here: 931 us
  blocking collectives  650 us (69%)
  waiting for transfers between devices  111 us (12%)
  matrix products  69.4 us (7%)
  local copies, waits for them, and re-layouts  58 us (6%)
  other arithmetic  29.5 us (3%)
  between operations  13.8 us (1%)
    psum x1, blocking collectives, head_total(): return lax.psum(partial_blocks, 'tp').astype(jnp.bfloat16)  650 us
    all_gather x1, waiting for transfers between devices, body(): lax.all_gather(out_rows, 'fsdp', axis=1, tiled=True)  42.8 us
    all_gather x1, waiting for transfers between devices, body(): lax.all_gather(query_cols, 'fsdp', axis=0, tiled=True)  40.6 us
    all_gather x1, waiting for transfers between devices, body(): lax.all_gather(value_cols, 'fsdp', axis=0, tiled=True)  22.1 us
    dot_general x1, matrix products, body(): jnp.dot(normed, lax.all_gather(query_cols, 'fsdp', axis=0, tiled=True), p...  19.5 us
  transfers between devices with their start and end apart: 4, of which 4 were waited for; matrix products, arithmetic and copies ran while one was open for 8% of the time, Pallas kernels for 0%

commit v1 on v0

v1 whole, which is shorter than its diff:
```python
import functools
import math

import jax
import jax.numpy as jnp
from jax import lax
from jax.experimental import pallas as pl
from jax.experimental.pallas import tpu as pltpu
from jax.sharding import PartitionSpec as P

HD = 128
STEPS = 4
GROUP = 4
LANES = 128
rope_base = 1000000.0
epsilon = 1e-06
masked = -1e30

MESH = pl.DeviceIdType.MESH
f32 = jnp.float32
bf16 = jnp.bfloat16

PROJ_JOBS = 6
OUT_JOBS = 4
JOBS = PROJ_JOBS + OUT_JOBS
BLOCK = 512
TOKENS = 512
CHUNKS = 4
CHUNK = TOKENS // CHUNKS
UNITS = 8
TP = 8
SENDS = 15


def al(x, m):
    return pl.multiple_of(x, m)


def layer_kernel(
    hidden, kcache, vcache, wq, wk, wv, wo, cos_ref, sin_ref, len_ref,
    out,
    wbuf, xn, kc, vc, qr, kn, vn, ctx, obuf, acc,
    gsend, grecv, csend, crecv, osend, orecv, local_sem,
):
    f, t = lax.axis_index("fsdp"), lax.axis_index("tp")
    z, lo, c = f // 4, (f // 2) % 2, f % 2
    y, hi = t // 2, t % 2
    c_is_hi = c == hi

    def dev(zz=z, ll=lo, cc=c, yy=y, hh=hi):
        return (zz * 4 + ll * 2 + cc, yy * 2 + hh)

    zp, zm = (z + 1) % 4, (z + 3) % 4
    yp, ym = (y + 1) % 4, (y + 3) % 4
    d_zp, d_zm = dev(zz=zp), dev(zz=zm)
    d_yp, d_ym = dev(yy=yp), dev(yy=ym)
    d_pair, d_hi, d_sib = dev(ll=1 - lo), dev(hh=1 - hi), dev(cc=1 - c)
    d_cross = dev(ll=1 - lo, hh=1 - hi)
    d_cross_sib = dev(ll=1 - lo, hh=1 - hi, cc=1 - c)

    def remote(src, dst, ssem, rsem, device):
        return pltpu.make_async_remote_copy(
            src_ref=src, dst_ref=dst, send_sem=ssem, recv_sem=rsem, device_id=device, device_id_type=MESH
        )

    xload = pltpu.make_async_copy(hidden.reshape(TOKENS, hidden.shape[2]), xn, local_sem.at[0])
    kload = pltpu.make_async_copy(kcache, kc, local_sem.at[1])
    vload = pltpu.make_async_copy(vcache, vc, local_sem.at[2])
    xload.start()

    def slot(j, zz, ll, cc):
        return wbuf.at[j, pl.ds(al(((zz * 2 + ll) * 2 + cc) * BLOCK, BLOCK), BLOCK)]

    place = (
        (z, lo), (zp, lo), (zm, lo), (z, 1 - lo), (zp, 1 - lo), (zm, 1 - lo), ((z + 2) % 4, lo), ((z + 2) % 4, 1 - lo)
    )

    def held(j, kind, cc=c):
        return slot(j, place[kind][0], place[kind][1], cc)

    def gput(j, index, src, dst, kind, device):
        remote(src, dst, gsend.at[j, index], grecv.at[j, kind], device).start()

    def gput_same(j, index, ref, kind, device):
        gput(j, index, ref, ref, kind, device)

    def gwait(j, kind):
        ref = held(j, kind % 8, c if kind < 8 else 1 - c)
        remote(ref, ref, gsend.at[j, 0], grecv.at[j, kind], d_sib).wait_recv()

    def first_a(j):
        def proj(source, width, head):
            def cols(tt):
                return source.at[:, pl.ds(al(tt * width + head * LANES, LANES), LANES)]

            pltpu.make_async_copy(cols(t), held(j, 0), grecv.at[j, 0]).start()
            gput(j, 2, cols(y * 2 + 1 - hi), held(j, 0), 3, d_cross)

        @pl.when(j == 0)
        def _():
            proj(wk, LANES, 0)

        @pl.when(j == 1)
        def _():
            proj(wv, LANES, 0)

        @pl.when(jnp.logical_and(j >= 2, j < PROJ_JOBS))
        def _():
            proj(wq, GROUP * LANES, j - 2)

        @pl.when(j >= PROJ_JOBS)
        def _():
            def rows(half):
                return wo.at[
                    pl.ds(al(half * 2048 + (j - PROJ_JOBS) * BLOCK, BLOCK), BLOCK), pl.ds(al(y * LANES, LANES), LANES)
                ]

            @pl.when(c_is_hi)
            def _():
                pltpu.make_async_copy(rows(c), held(j, 0), grecv.at[j, 0]).start()
                pltpu.make_async_copy(rows(1 - c), held(j, 0, 1 - c), grecv.at[j, 8]).start()
                gput(j, 2, rows(1 - c), held(j, 0, 1 - c), 0, d_sib)
                gput(j, 7, rows(c), held(j, 0), 8, d_sib)

            @pl.when(jnp.logical_not(c_is_hi))
            def _():
                gput(j, 2, rows(c), held(j, 0), 3, d_cross)
                gput(j, 7, rows(1 - c), held(j, 0, 1 - c), 3, d_cross_sib)

    def first_b(j):
        gwait(j, 0)
        own = held(j, 0)
        gput_same(j, 0, own, 2, d_zp)
        gput_same(j, 1, own, 1, d_zm)

        @pl.when(j < PROJ_JOBS)
        def _():
            gput_same(j, 7, own, 8, d_sib)

    def to_sib(j, kind):
        gput_same(j, 7 + kind, held(j, kind), 8 + kind, d_sib)

    def mid1(j):
        even = j % 2 == 0
        gwait(j, 1)
        gput_same(j, 3, held(j, 1), 4, d_pair)

        @pl.when(even)
        def _():
            gput_same(j, 5, held(j, 1), 6, d_zm)

        to_sib(j, 1)
        gwait(j, 2)
        gput_same(j, 4, held(j, 2), 5, d_pair)

        @pl.when(jnp.logical_not(even))
        def _():
            gput_same(j, 5, held(j, 2), 6, d_zp)

        to_sib(j, 2)
        gwait(j, 3)
        to_sib(j, 3)

    def mid2(j):
        even = j % 2 == 0
        gwait(j, 4)

        @pl.when(even)
        def _():
            gput_same(j, 6, held(j, 4), 7, d_zm)

        to_sib(j, 4)
        gwait(j, 5)

        @pl.when(jnp.logical_not(even))
        def _():
            gput_same(j, 6, held(j, 5), 7, d_zp)

        to_sib(j, 5)
        gwait(j, 6)
        to_sib(j, 6)

    def fin(j):
        gwait(j, 7)
        to_sib(j, 7)
        for kind in range(8, 16):
            gwait(j, kind)

    def gdone(j):
        for index in range(SENDS):
            ref = held(j, 0)
            remote(ref, ref, gsend.at[j, index], grecv.at[j, 0], d_sib).wait_send()

    y2 = (y + 2) % 4
    peer = ((y, hi), (yp, hi), (ym, hi), (y, 1 - hi), (yp, 1 - hi), (ym, 1 - hi), (y2, hi), (y2, 1 - hi))

    class Ring:
        def __init__(self, ssem, rsem, ref_of):
            self.ssem, self.rsem, self.ref_of = ssem, rsem, ref_of

        def at(self, j, kind):
            return self.ref_of(j, peer[kind][0], peer[kind][1])

        def put(self, j, index, src, kind_here, kind, device):
            remote(src, self.at(j, kind_here), self.ssem.at[j, index], self.rsem.at[j, kind], device).start()

        def forward(self, j, index, kind_here, kind, device):
            self.put(j, index, self.at(j, kind_here), kind_here, kind, device)

        def wait(self, j, kind):
            ref = self.at(j, kind)
            remote(ref, ref, self.ssem.at[j, 0], self.rsem.at[j, kind], d_sib).wait_recv()

        def begin(self, j, src):
            self.put(j, 0, src, 0, 2, d_yp)
            self.put(j, 1, src, 0, 1, d_ym)
            self.put(j, 2, src, 0, 3, d_hi)

        def mid1(self, j):
            even = j % 2 == 0
            self.wait(j, 1)

            @pl.when(even)
            def _():
                self.forward(j, 3, 1, 6, d_ym)

            self.wait(j, 2)

            @pl.when(jnp.logical_not(even))
            def _():
                self.forward(j, 3, 2, 6, d_yp)

            self.wait(j, 3)
            self.forward(j, 4, 3, 5, d_yp)
            self.forward(j, 5, 3, 4, d_ym)

        def mid2(self, j):
            self.wait(j, 6)
            self.forward(j, 6, 6, 7, d_hi)
            self.wait(j, 4)
            self.wait(j, 5)

        def fin(self, j):
            self.wait(j, 7)

        def done(self, j):
            ref = self.at(j, 0)
            for index in range(7):
                remote(ref, ref, self.ssem.at[j, index], self.rsem.at[j, 1], d_sib).wait_send()

    out2 = out.reshape(TOKENS, out.shape[2])

    def ctx_block(j, yy, hh):
        return ctx.at[yy * 2 + hh, pl.ds(al(j * CHUNK, CHUNK), CHUNK)]

    def out_block(j, yy, hh):
        return out2.at[:, pl.ds(al((j * 2 + hh) * 512 + yy * LANES, LANES), LANES)]

    ctx_ring = Ring(csend, crecv, ctx_block)
    out_ring = Ring(osend, orecv, out_block)

    def norm(i):
        rows = pl.ds(al(i * 64, 64), 64)
        width = xn.shape[1]

        def square(k, total):
            v = xn[rows, pl.ds(al(k * 512, 512), 512)].astype(f32)
            v = v * v
            return total + (v[:, :128] + v[:, 128:256]) + (v[:, 256:384] + v[:, 384:])

        total = lax.fori_loop(0, width // 512, square, jnp.zeros((64, 128), f32))
        scale = lax.rsqrt(jnp.sum(total, axis=1, keepdims=True) * (1.0 / width) + epsilon)

        def apply(k, _):
            cols = pl.ds(al(k * 512, 512), 512)
            xn[rows, cols] = (xn[rows, cols].astype(f32) * scale).astype(bf16)
            return 0

        lax.fori_loop(0, width // 512, apply, 0)

    def project(j):
        acc[...] = jnp.zeros_like(acc)

        def part(k, _):
            cols = pl.ds(al(k * 1024, 1024), 1024)
            acc[...] += jnp.dot(xn[:, cols], wbuf[j, cols, :], preferred_element_type=f32)
            return 0

        lax.fori_loop(0, 8, part, 0)

        @pl.when(j == 1)
        def _():
            vn[...] = acc[...].astype(bf16)

        @pl.when(j != 1)
        def _():
            v = acc[...]
            rotated = (v * cos_ref[...] + pltpu.roll(v, HD // 2, 1) * sin_ref[...]).astype(bf16)

            @pl.when(j == 0)
            def _():
                kn[...] = rotated

            @pl.when(j >= 2)
            def _():
                qr[j - 2] = rotated

    scaling = 1.0 / math.sqrt(HD)
    nt = (((1,), (1,)), ((), ()))

    def attend(i):
        def block(b, _):
            tok = al(i * CHUNK + b * 16, 16)
            q = jnp.concatenate([qr[g, pl.ds(tok, 16), :] for g in range(GROUP)], axis=0)
            slots = pl.ds(al((i * 32 + b * 4) * 128, 512), 512)
            fresh = pl.ds(al(i * CHUNK, CHUNK), CHUNK)
            older = lax.dot_general(q, kc[slots, :], nt, preferred_element_type=f32) * scaling
            recent = lax.dot_general(q, kn[fresh, :], nt, preferred_element_type=f32) * scaling
            live = len_ref[pl.ds(tok, 16), :1]
            live = jnp.concatenate([live] * GROUP, axis=0)
            token = lax.broadcasted_iota(jnp.int32, (16 * GROUP, 1), 0) % 16
            row = token // STEPS
            lane = lax.broadcasted_iota(jnp.int32, older.shape, 1)
            older = jnp.where((lane >= row * 128) & (lane < row * 128 + live), older, masked)
            lane = lax.broadcasted_iota(jnp.int32, recent.shape, 1) - b * 16
            recent = jnp.where((lane >= row * STEPS) & (lane <= token), recent, masked)
            highest = jnp.maximum(jnp.max(older, axis=1, keepdims=True), jnp.max(recent, axis=1, keepdims=True))
            older = jnp.exp(older - highest)
            recent = jnp.exp(recent - highest)
            total = jnp.sum(older, axis=1, keepdims=True) + jnp.sum(recent, axis=1, keepdims=True)
            inverse = 1.0 / total
            mix = jnp.dot((older * inverse).astype(bf16), vc[slots, :], preferred_element_type=f32)
            mix += jnp.dot((recent * inverse).astype(bf16), vn[fresh, :], preferred_element_type=f32)
            mix = mix.astype(bf16)
            for g in range(GROUP):
                ctx[t, pl.ds(tok, 16), g * HD:(g + 1) * HD] = mix[g * 16:(g + 1) * 16]
            return 0

        lax.fori_loop(0, 8, block, 0)

    def out_unit(u):
        acc[...] = jnp.zeros_like(acc)

        def part(tt, _):
            weights = wbuf[PROJ_JOBS + tt % 4, pl.ds(al((u * 2 + tt // 4) * BLOCK, BLOCK), BLOCK), :]
            acc[...] += jnp.dot(ctx[tt], weights, preferred_element_type=f32)
            return 0

        lax.fori_loop(0, TP, part, 0)
        obuf[u] = acc[...].astype(bf16)

    barrier = pltpu.get_barrier_semaphore()
    partners = (d_zp, d_zm, d_yp, d_ym, d_pair, d_hi, d_sib, d_cross, d_cross_sib)
    for device in partners:
        pl.semaphore_signal(barrier, inc=1, device_id=device, device_id_type=MESH)
    pl.semaphore_wait(barrier, len(partners))

    first_a(jnp.int32(0))
    first_a(jnp.int32(1))
    kload.start()
    vload.start()
    first_b(jnp.int32(0))
    xload.wait()

    def within(j, low, high, run):
        @pl.when(jnp.logical_and(j >= low, j < high))
        def _():
            run(j)

    steps = JOBS + 2

    def step(s, _):
        within(s + 2, 0, JOBS, first_a)
        within(s + 1, 0, JOBS, first_b)

        @pl.when(s < 2)
        def _():
            def some(i, _):
                norm(s * 4 + i)
                return 0

            lax.fori_loop(0, 4, some, 0)

        within(s, 0, JOBS, mid1)
        within(s - 1, 0, JOBS, mid2)
        within(s - 2, 0, JOBS, fin)
        within(s - 2, 0, PROJ_JOBS, project)

        @pl.when(s == PROJ_JOBS + 2)
        def _():
            kload.wait()
            vload.wait()

        @pl.when(jnp.logical_and(s >= PROJ_JOBS + 2, s < PROJ_JOBS + 2 + CHUNKS))
        def _():
            i = s - (PROJ_JOBS + 2)
            attend(i)
            ctx_ring.begin(i, ctx_block(i, y, hi))

        within(s - (PROJ_JOBS + 3), 0, CHUNKS, ctx_ring.mid1)
        within(s - (PROJ_JOBS + 4), 0, CHUNKS, ctx_ring.mid2)
        within(s - (PROJ_JOBS + 5), 0, CHUNKS, ctx_ring.fin)
        within(s - 4, 0, JOBS, gdone)
        return 0

    lax.fori_loop(0, steps, step, 0)
    ctx_ring.mid1(CHUNKS - 1)
    ctx_ring.mid2(CHUNKS - 2)
    ctx_ring.fin(CHUNKS - 3)
    ctx_ring.mid2(CHUNKS - 1)
    ctx_ring.fin(CHUNKS - 2)
    ctx_ring.fin(CHUNKS - 1)

    def ostep(u, _):
        @pl.when(u < UNITS)
        def _():
            out_unit(u)
            pltpu.make_async_copy(obuf.at[u], out_ring.at(u, 0), local_sem.at[3 + u]).start()
            out_ring.begin(u, obuf.at[u])

        within(u - 1, 0, UNITS, out_ring.mid1)
        within(u - 2, 0, UNITS, out_ring.mid2)
        within(u - 3, 0, UNITS, out_ring.fin)
        within(u - 3, 0, UNITS, out_ring.done)
        return 0

    lax.fori_loop(0, UNITS + 3, ostep, 0)
    for u in range(UNITS):
        pltpu.make_async_copy(obuf.at[u], out_ring.at(u, 0), local_sem.at[3 + u]).wait()
    for j in range(steps - 4, JOBS):
        gdone(j)
    for j in range(CHUNKS):
        ctx_ring.done(j)


def body(
    hidden_in, lengths, key_cache, value_cache, query_weight, key_weight, value_weight, out_weight
):
    row_count, step_count, width = hidden_in.shape
    slots = key_cache.shape[1]
    offsets = lax.broadcasted_iota(jnp.int32, (row_count, step_count), 1)
    positions = (lengths[:, None] + offsets).reshape(TOKENS)
    frequency = rope_base ** (-(jnp.arange(HD // 2, dtype=f32) * 2.0) / HD)
    angles = positions.astype(f32)[:, None] * frequency
    cosine, sine = jnp.cos(angles), jnp.sin(angles)
    cosine = jnp.concatenate([cosine, cosine], axis=1)
    sine = jnp.concatenate([-sine, sine], axis=1)
    live = jnp.broadcast_to(jnp.repeat(lengths, step_count)[:, None], (TOKENS, LANES))
    hbm = pl.BlockSpec(memory_space=pl.ANY)
    vmem = pl.BlockSpec(memory_space=pltpu.VMEM)
    dma = pltpu.SemaphoreType.DMA
    return pl.pallas_call(
        layer_kernel,
        out_shape=jax.ShapeDtypeStruct(hidden_in.shape, bf16),
        in_specs=[hbm] * 7 + [vmem] * 3,
        out_specs=hbm,
        scratch_shapes=[
            pltpu.VMEM((JOBS, width, LANES), bf16),
            pltpu.VMEM((TOKENS, width), bf16),
            pltpu.VMEM((row_count * slots, HD), bf16),
            pltpu.VMEM((row_count * slots, HD), bf16),
            pltpu.VMEM((GROUP, TOKENS, HD), bf16),
            pltpu.VMEM((TOKENS, HD), bf16),
            pltpu.VMEM((TOKENS, HD), bf16),
            pltpu.VMEM((TP, TOKENS, GROUP * HD), bf16),
            pltpu.VMEM((UNITS, TOKENS, LANES), bf16),
            pltpu.VMEM((TOKENS, LANES), f32),
            dma((JOBS, SENDS)),
            dma((JOBS, 16)),
            dma((CHUNKS, 7)),
            dma((CHUNKS, 8)),
            dma((UNITS, 7)),
            dma((UNITS, 8)),
            dma((3 + UNITS,)),
        ],
        compiler_params=pltpu.CompilerParams(
            collective_id=0, has_side_effects=True, vmem_limit_bytes=60 * 1024 * 1024
        ),
        name="attention_layer",
    )(
        hidden_in,
        key_cache.reshape(row_count * slots, HD),
        value_cache.reshape(row_count * slots, HD),
        query_weight, key_weight, value_weight, out_weight, cosine, sine, live,
    )


def solution(mesh):
    return jax.shard_map(
        body,
        mesh=mesh,
        in_specs=(
            P("fsdp", None, None),
            P("fsdp"),
            P("fsdp", None, "tp"),
            P("fsdp", None, "tp"),
            P("fsdp", None),
            P("fsdp", None),
            P("fsdp", None),
            P(None, "fsdp"),
        ),
        out_specs=P("fsdp", None, None),
        check_vma=False,
    )
```

time: 938 us -> 195 us (0.21)
  blocking collectives: 650 us -> 0 us
  Pallas kernels: 0 us -> 183 us
  waiting for transfers between devices: 111 us -> 0 us
  matrix products: 69.4 us -> 0 us
  local copies, waits for them, and re-layouts: 58 us -> 9.93 us
  other arithmetic: 29.5 us -> 2.02 us
  between operations: 13.8 us -> 0.04 us
    psum x1 -> x0, blocking collectives: 650 us -> none  [head_total(): return lax.psum(partial_blocks, 'tp').astype(jnp.bfloat16)]
    pallas_call x0 -> x1, Pallas kernels: none -> 183 us  [body(): pl.pallas_call(layer_kernel, out_shape=jax.ShapeDtypeStruct(hidden_in.sha...]
    all_gather x4 -> x0, waiting for transfers between devices: 111 us -> none  [the longest x1 42.8 us: body(): lax.all_gather(out_rows, 'fsdp', axis=1, tiled=True)]
    dot_general x8 -> x0, matrix products: 69.4 us -> none  [the longest x1 19.5 us: body(): jnp.dot(normed, lax.all_gather(query_cols, 'fsdp', axis=0, tiled=True), p...]
    dot_general x2 -> x0, local copies, waits for them, and re-layouts: 23.9 us -> none  [the longest x1 12 us: body(): jnp.dot(context, lax.all_gather(out_rows, 'fsdp', axis=1, tiled=True), pr...]
    convert_element_type x3 -> x1, other arithmetic: 17.2 us -> 0.01 us  [body(): angles = positions.astype(f32)[:, None] * frequency]
    another operation x1 -> x0, local copies, waits for them, and re-layouts: 14.5 us -> none  [body(): return result.reshape(row_count, step_count, model_width)]
    convert_element_type x1 -> x0, local copies, waits for them, and re-layouts: 11.4 us -> none  [head_total(): return lax.psum(partial_blocks, 'tp').astype(jnp.bfloat16)]
  transfers between devices with their start and end apart: 4 -> 0, of which waited for: 4 -> 0; matrix products, arithmetic and copies ran while one was open for 8% -> 0% of each run, Pallas kernels for 0% -> 0%
where the time goes in v1:
time: 195 us
  Pallas kernels  183 us (94%)
  local copies, waits for them, and re-layouts  9.93 us (5%)
  other arithmetic  2.02 us (1%)
    pallas_call x1, Pallas kernels, body(): pl.pallas_call(layer_kernel, out_shape=jax.ShapeDtypeStruct(hidden_in.sha...  183 us
    unnamed x1, local copies, waits for them, and re-layouts  8.14 us

profile of v1, /device:TPU:0, one launch (start us, length us, event | category | flops | bytes accessed | tf_op | source)
XLA Modules:
  0.0 194.7 jit_solution(17568994874470299623)
XLA Ops:
  0.0 0.7 add.15
  0.7 0.1 add.16
  0.9 0.1 iota.15
  1.0 0.8 broadcast_in_dim.2.len_ref
  1.8 1.0 fusion
  2.8 1.0 pad_maximum_fusion
  3.8 182.7 %attention_layer.1 = bf16[128,4,8192]{2,1,0:T(4,128)(2,1)} custom-call(bf16[128,4,8192]{2,1,0:T(4,128)(2,1)} %hidden.1, bf16[16384,128]{1,0:T(8,128)(2,1)} %bitcast.2, bf16[16384,128]{1,0:T(8,128)(2,1)} %bitcast.3, bf16[512,4096]{1,0:T(8,128)(2,1)} %wq.1, bf16[512,1024]{1,0:T(8,128)(2,1)} %wk.1, bf16[512,1024]{1,0:T(8,128)(2,1)} %wv.1, ...), custom_call_target="tpu_custom_call" | custom-call | tf_op jit(solution)/shard_map/attention_layer/pallas_call | solution.py:452
  186.6 8.1 %copy.10 = bf16[128,4,8192]{2,1,0:T(4,128)(2,1)} copy(bf16[128,4,8192]{2,1,0:T(4,128)(2,1)} %attention_layer.1) | data formatting | bytes 16777216
  (3 shorter events, 0.0 us)

commit v2 on v0

v2 whole, which is shorter than its diff:
```python
import math

import jax
import jax.numpy as jnp
import numpy as np
from jax import lax
from jax.experimental import pallas as pl
from jax.experimental.pallas import tpu as pltpu
from jax.sharding import PartitionSpec as P

HD = 128
STEPS = 4
GROUP = 4
LANES = 128
rope_base = 1000000.0
epsilon = 1e-06
masked = -1e30

MESH = pl.DeviceIdType.MESH
f32 = jnp.float32
bf16 = jnp.bfloat16

JOBS = 6
QUARTERS = 4
BLOCK = 512
TOKENS = 512
HALF = TOKENS // 2
TP = 8
UNITS = (0, 3, 1, 2, 4, 5, 6, 7)


def al(x, m):
    return pl.multiple_of(x, m)


def layer_kernel(
    hidden, kcache, vcache, wq, wk, wv, wo, lengths, frequency,
    out,
    wbuf, wobuf, xn, kc, vc, qr, kn, vn, ctx, acc, cos_ref, sin_ref, len_ref,
    gsend, grecv, gsib, wsend, wrecv, wsib, csend, crecv, osend, orecv, local_sem,
):
    f, t = lax.axis_index("fsdp"), lax.axis_index("tp")
    z, lo, c = f // 4, (f // 2) % 2, f % 2
    y, hi = t // 2, t % 2
    c_is_hi = c == hi

    def dev(zz=z, ll=lo, cc=c, yy=y, hh=hi):
        return (zz * 4 + ll * 2 + cc, yy * 2 + hh)

    zp, zm, z2 = (z + 1) % 4, (z + 3) % 4, (z + 2) % 4
    yp, ym, y2 = (y + 1) % 4, (y + 3) % 4, (y + 2) % 4
    d_zp, d_zm = dev(zz=zp), dev(zz=zm)
    d_yp, d_ym = dev(yy=yp), dev(yy=ym)
    d_pair, d_hi, d_sib = dev(ll=1 - lo), dev(hh=1 - hi), dev(cc=1 - c)
    d_cross = dev(ll=1 - lo, hh=1 - hi)
    d_cross_sib = dev(ll=1 - lo, hh=1 - hi, cc=1 - c)

    def remote(src, dst, ssem, rsem, device):
        return pltpu.make_async_remote_copy(
            src_ref=src, dst_ref=dst, send_sem=ssem, recv_sem=rsem, device_id=device, device_id_type=MESH
        )

    place = ((z, lo), (zp, lo), (zm, lo), (z, 1 - lo), (zp, 1 - lo), (zm, 1 - lo), (z2, lo), (z2, 1 - lo))

    def group(kind):
        return (0, 1, 1, 0, 2, 2, 3, 3)[kind]

    class Gather:
        def __init__(self, buffer, ssem, rsem, sib_sem):
            self.buffer, self.ssem, self.rsem, self.sib_sem = buffer, ssem, rsem, sib_sem

        def held(self, j, kind, cc=c):
            zz, ll = place[kind]
            return self.buffer.at[j, pl.ds(al(((zz * 2 + ll) * 2 + cc) * BLOCK, BLOCK), BLOCK)]

        def load(self, j, src, kind):
            if kind < 8:
                pltpu.make_async_copy(src, self.held(j, kind), self.rsem.at[j, kind]).start()
            else:
                pltpu.make_async_copy(src, self.held(j, kind - 8, 1 - c), self.sib_sem(j, kind - 8)).start()

        def put(self, j, src, dst, kind, device):
            sem = self.rsem.at[j, kind] if kind < 8 else self.sib_sem(j, kind - 8)
            remote(src, dst, self.ssem.at[j], sem, device).start()

        def pass_on(self, j, kind_here, kind, device):
            ref = self.held(j, kind_here)
            self.put(j, ref, ref, kind, device)

        def to_sib(self, j, kind):
            self.pass_on(j, kind, 8 + kind, d_sib)

        def wait(self, j, kind):
            ref = self.held(j, kind)
            remote(ref, ref, self.ssem.at[j], self.rsem.at[j, kind], d_sib).wait_recv()

        def wait_sib(self, sem):
            ref = self.buffer.at[0, pl.ds(0, 8 * BLOCK)]
            remote(ref, ref, self.ssem.at[0], sem, d_sib).wait_recv()

        def sent(self, j, count):
            ref = self.buffer.at[j, pl.ds(0, count * BLOCK)]
            remote(ref, ref, self.ssem.at[j], self.rsem.at[j, 0], d_sib).wait_send()

    proj = Gather(wbuf, gsend, grecv, lambda j, kind: gsib.at[j])
    outw = Gather(wobuf, wsend, wrecv, lambda q, kind: wsib.at[group(kind)])

    def source_of(j):
        return ((wk, LANES, 0), (wv, LANES, 0))[j] if j < 2 else (wq, GROUP * LANES, j - 2)

    def first_a(j):
        source, width, head = source_of(j)
        proj.load(j, source.at[:, pl.ds(al(t * width + head * LANES, LANES), LANES)], 0)

    def first_x(j):
        source, width, head = source_of(j)
        cols = source.at[:, pl.ds(al((y * 2 + 1 - hi) * width + head * LANES, LANES), LANES)]
        proj.put(j, cols, proj.held(j, 0), 3, d_cross)

    def first_b(j):
        proj.wait(j, 0)
        proj.pass_on(j, 0, 2, d_zp)
        proj.pass_on(j, 0, 1, d_zm)
        proj.to_sib(j, 0)

    def mid1(j):
        proj.wait(j, 1)
        proj.pass_on(j, 1, 4, d_pair)
        proj.wait(j, 2)
        proj.pass_on(j, 2, 5, d_pair)
        if j % 2 == 0:
            proj.pass_on(j, 1, 6, d_zm)
        else:
            proj.pass_on(j, 2, 6, d_zp)
        proj.to_sib(j, 1)
        proj.to_sib(j, 2)
        proj.wait(j, 3)
        proj.to_sib(j, 3)

    def mid2(j):
        proj.wait(j, 4)
        if j % 2 == 0:
            proj.pass_on(j, 4, 7, d_zm)
        proj.to_sib(j, 4)
        proj.wait(j, 5)
        if j % 2 == 1:
            proj.pass_on(j, 5, 7, d_zp)
        proj.to_sib(j, 5)
        proj.wait(j, 6)
        proj.to_sib(j, 6)

    def fin(j):
        proj.wait(j, 7)
        proj.to_sib(j, 7)
        proj.wait_sib(gsib.at[j])

    def ow_rows(q, half):
        return wo.at[pl.ds(al(half * 2048 + q * BLOCK, BLOCK), BLOCK), pl.ds(al(y * LANES, LANES), LANES)]

    def ow_load():
        for q in range(QUARTERS):
            @pl.when(c_is_hi)
            def _():
                outw.load(q, ow_rows(q, c), 0)
                outw.load(q, ow_rows(q, 1 - c), 8)
                outw.put(q, ow_rows(q, 1 - c), outw.held(q, 0, 1 - c), 0, d_sib)
                outw.put(q, ow_rows(q, c), outw.held(q, 0), 8, d_sib)

    def ow_first():
        for q in range(QUARTERS):
            outw.wait(q, 0)
            outw.pass_on(q, 0, 2, d_zp)
            outw.pass_on(q, 0, 1, d_zm)
            if q % 2 == 0:
                outw.pass_on(q, 0, 3, d_pair)
            else:
                @pl.when(jnp.logical_not(c_is_hi))
                def _():
                    outw.put(q, ow_rows(q, c), outw.held(q, 0), 3, d_cross)
                    outw.put(q, ow_rows(q, 1 - c), outw.held(q, 0, 1 - c), 3, d_cross_sib)

    def ow_second():
        for q in range(QUARTERS):
            outw.wait(q, 3)
            outw.pass_on(q, 3, 5, d_zp)
            outw.pass_on(q, 3, 4, d_zm)
            outw.to_sib(q, 3)
        for q in range(QUARTERS):
            for kind in (1, 2):
                outw.wait(q, kind)
                outw.to_sib(q, kind)
            if q % 2 == 0:
                outw.pass_on(q, 1, 6, d_zm)
            else:
                outw.pass_on(q, 2, 6, d_zp)

    def ow_third():
        for q in range(QUARTERS):
            for kind in (4, 5):
                outw.wait(q, kind)
                outw.to_sib(q, kind)
            if q % 2 == 0:
                outw.pass_on(q, 4, 7, d_zm)
            else:
                outw.pass_on(q, 5, 7, d_zp)

    def ow_last():
        for q in range(QUARTERS):
            for kind in (6, 7):
                outw.wait(q, kind)
                outw.to_sib(q, kind)

    def ow_ready(i):
        outw.wait_sib(wsib.at[i])

    peer = ((y, hi), (yp, hi), (ym, hi), (y, 1 - hi), (yp, 1 - hi), (ym, 1 - hi), (y2, hi), (y2, 1 - hi))

    class Ring:
        def __init__(self, ssem, rsem, block, seven):
            self.ssem, self.rsem, self.block, self.seven = ssem, rsem, block, seven

        def at(self, j, kind):
            return self.block(j, peer[kind][0], peer[kind][1])

        def forward(self, j, kind_here, kind, device):
            ref = self.at(j, kind_here)
            remote(ref, ref, self.ssem.at[j], self.rsem.at[j, kind], device).start()

        def wait(self, j, kind):
            ref = self.at(j, kind)
            remote(ref, ref, self.ssem.at[j], self.rsem.at[j, kind], d_sib).wait_recv()

        def begin(self, j):
            self.forward(j, 0, 2, d_yp)
            self.forward(j, 0, 1, d_ym)
            self.forward(j, 0, 3, d_hi)

        def mid1(self, j):
            self.wait(j, 1)
            if j % 2 == 0:
                self.forward(j, 1, 6, d_ym)
            self.wait(j, 2)
            if j % 2 == 1:
                self.forward(j, 2, 6, d_yp)
            self.wait(j, 3)
            self.forward(j, 3, 5, d_yp)
            self.forward(j, 3, 4, d_ym)

        def mid2(self, j):
            self.wait(j, 6)
            self.forward(j, 6, 7, d_hi)
            self.wait(j, 4)
            self.wait(j, 5)

        def fin(self, j):
            self.wait(j, 7)

        def done(self, j):
            remote(self.seven, self.seven, self.ssem.at[j], self.rsem.at[j, 1], d_sib).wait_send()

    def ctx_block(j, yy, hh):
        return ctx.at[yy * 2 + hh, j // 2, pl.ds((j % 2) * HALF, HALF)]

    def out_cols(j, yy, hh):
        zz, ll = place[UNITS[j]]
        return pl.ds(al(((zz * 2 + ll) * 2 + hh) * BLOCK + yy * LANES, LANES), LANES)

    def out_block(j, yy, hh):
        return out.at[:, out_cols(j, yy, hh)]

    ctx_ring = Ring(csend, crecv, ctx_block, ctx.at[pl.ds(0, 7), 0, pl.ds(0, HALF)])
    out_ring = Ring(osend, orecv, out_block, out.at[:, pl.ds(0, 7 * LANES)])

    def tables():
        def part(i, _):
            rows = pl.ds(al(i * 64, 64), 64)
            token = lax.broadcasted_iota(jnp.int32, (64, LANES), 0) + i * 64
            lane = lax.broadcasted_iota(jnp.int32, (64, LANES), 1)
            mine = jnp.where(lane == token // STEPS, lengths[...].astype(f32), 0.0)
            live = jnp.sum(mine, axis=1, keepdims=True)
            len_ref[rows, :] = jnp.broadcast_to(live, (64, LANES)).astype(jnp.int32)
            angles = (live + (token % STEPS).astype(f32)) * frequency[...]
            cos_ref[rows, :] = jnp.cos(angles)
            sine = jnp.sin(angles)
            sin_ref[rows, :] = jnp.where(lane < HD // 2, -sine, sine)
            return 0

        lax.fori_loop(0, TOKENS // 64, part, 0)

    def norm(i, _):
        rows = pl.ds(al(i * 64, 64), 64)
        width = xn.shape[1]

        def square(k, total):
            v = xn[rows, pl.ds(al(k * 512, 512), 512)].astype(f32)
            v = v * v
            return total + (v[:, :128] + v[:, 128:256]) + (v[:, 256:384] + v[:, 384:])

        total = lax.fori_loop(0, width // 512, square, jnp.zeros((64, 128), f32))
        scale = lax.rsqrt(jnp.sum(total, axis=1, keepdims=True) * (1.0 / width) + epsilon)

        def apply(k, _):
            cols = pl.ds(al(k * 512, 512), 512)
            xn[rows, cols] = (xn[rows, cols].astype(f32) * scale).astype(bf16)
            return 0

        lax.fori_loop(0, width // 512, apply, 0)
        return 0

    def project(p):
        acc[...] = jnp.zeros_like(acc)

        def part(k, _):
            cols = pl.ds(al(k * 1024, 1024), 1024)
            weights = jnp.concatenate([wbuf[2 * p, cols, :], wbuf[2 * p + 1, cols, :]], axis=1)
            acc[...] += jnp.dot(xn[:, cols], weights, preferred_element_type=f32)
            return 0

        lax.fori_loop(0, 8, part, 0)

        def rotated(v):
            return (v * cos_ref[...] + pltpu.roll(v, HD // 2, 1) * sin_ref[...]).astype(bf16)

        if p == 0:
            kn[...] = rotated(acc[:, :HD])
            vn[...] = acc[:, HD:].astype(bf16)
        else:
            qr[2 * p - 2] = rotated(acc[:, :HD])
            qr[2 * p - 1] = rotated(acc[:, HD:])

    scaling = 1.0 / math.sqrt(HD)
    nt = (((1,), (1,)), ((), ()))

    def attend(p, i):
        fresh = slice(i * 128, (i + 1) * 128)
        token = lax.broadcasted_iota(jnp.int32, (32, 1), 0) % 16
        row = token // STEPS
        scores = []
        for b in range(8):
            tok = slice(i * 128 + b * 16, i * 128 + (b + 1) * 16)
            q = jnp.concatenate([qr[2 * p, tok, :], qr[2 * p + 1, tok, :]], axis=0)
            keys = kc[(i * 8 + b) * 512:(i * 8 + b + 1) * 512, :]
            older = lax.dot_general(q, keys, nt, preferred_element_type=f32) * scaling
            recent = lax.dot_general(q, kn[fresh, :], nt, preferred_element_type=f32) * scaling
            scores.append((older, recent))
        for b in range(8):
            older, recent = scores[b]
            live = len_ref[i * 128 + b * 16:i * 128 + (b + 1) * 16, :1]
            live = jnp.concatenate([live, live], axis=0)
            lane = lax.broadcasted_iota(jnp.int32, older.shape, 1)
            older = jnp.where((lane >= row * 128) & (lane < row * 128 + live), older, masked)
            lane = lax.broadcasted_iota(jnp.int32, recent.shape, 1) - b * 16
            recent = jnp.where((lane >= row * STEPS) & (lane <= token), recent, masked)
            scores[b] = older, recent
        highest = [
            jnp.maximum(jnp.max(older, axis=1, keepdims=True), jnp.max(recent, axis=1, keepdims=True))
            for older, recent in scores
        ]
        scores = [(jnp.exp(older - h), jnp.exp(recent - h)) for (older, recent), h in zip(scores, highest)]
        inverse = [
            1.0 / (jnp.sum(older, axis=1, keepdims=True) + jnp.sum(recent, axis=1, keepdims=True))
            for older, recent in scores
        ]
        mixes = []
        for b in range(8):
            older, recent = scores[b]
            values = vc[(i * 8 + b) * 512:(i * 8 + b + 1) * 512, :]
            mix = jnp.dot((older * inverse[b]).astype(bf16), values, preferred_element_type=f32)
            mix += jnp.dot((recent * inverse[b]).astype(bf16), vn[fresh, :], preferred_element_type=f32)
            mixes.append(mix.astype(bf16))
        for b in range(8):
            tok = slice(i * 128 + b * 16, i * 128 + (b + 1) * 16)
            ctx[t, p, tok, :] = jnp.concatenate([mixes[b][:16], mixes[b][16:]], axis=1)

    def out_units(j):
        acc[...] = jnp.zeros_like(acc)
        slots = [(place[UNITS[j + i]][0] * 2 + place[UNITS[j + i]][1]) * 2 for i in range(2)]

        def part(i, _):
            def weights(tt):
                half = tt // 4
                pieces = [wobuf[tt % 4, pl.ds(al((slot + half) * BLOCK, BLOCK), BLOCK), :] for slot in slots]
                return jnp.concatenate(pieces, axis=1)

            left = jnp.concatenate([ctx[2 * i, 0], ctx[2 * i, 1], ctx[2 * i + 1, 0], ctx[2 * i + 1, 1]], axis=1)
            right = jnp.concatenate([weights(2 * i), weights(2 * i + 1)], axis=0)
            acc[...] += jnp.dot(left, right, preferred_element_type=f32)
            return 0

        lax.fori_loop(0, TP // 2, part, 0)
        for i in range(2):
            out[:, out_cols(j + i, y, hi)] = acc[:, i * LANES:(i + 1) * LANES].astype(bf16)

    xload = pltpu.make_async_copy(hidden.reshape(TOKENS, hidden.shape[2]), xn, local_sem.at[0])
    kload = pltpu.make_async_copy(kcache, kc, local_sem.at[1])
    vload = pltpu.make_async_copy(vcache, vc, local_sem.at[2])
    barrier = pltpu.get_barrier_semaphore()
    partners = (d_hi, d_zp, d_zm, d_yp, d_ym, d_pair, d_cross, d_cross_sib, d_sib)
    for device in partners:
        pl.semaphore_signal(barrier, inc=1, device_id=device, device_id_type=MESH)
    for j in range(3):
        first_a(j)
    xload.start()
    kload.start()
    vload.start()
    tables()
    pl.semaphore_wait(barrier, len(partners))
    for j in range(2):
        first_x(j)
        first_b(j)
    xload.wait()
    lax.fori_loop(0, TOKENS // 64, norm, 0)
    for j in range(4):
        mid1(j)
        first_x(j + 2)
        first_b(j + 2)
        if j < 3:
            first_a(j + 3)
        if j >= 1:
            mid2(j - 1)
        if j >= 2:
            fin(j - 2)
    project(0)
    mid1(4)
    mid2(3)
    fin(2)
    ow_load()
    mid1(5)
    mid2(4)
    fin(3)
    project(1)
    kload.wait()
    vload.wait()
    mid2(5)
    ow_first()
    attend(0, 0)
    attend(0, 1)
    ctx_ring.begin(0)
    fin(4)
    attend(0, 2)
    attend(0, 3)
    ctx_ring.begin(1)
    fin(5)
    project(2)
    ctx_ring.mid1(0)
    attend(1, 0)
    attend(1, 1)
    ctx_ring.begin(2)
    ctx_ring.mid1(1)
    attend(1, 2)
    attend(1, 3)
    ctx_ring.begin(3)
    ow_second()
    ctx_ring.mid2(0)
    ctx_ring.mid1(2)
    ctx_ring.mid2(1)
    ctx_ring.mid1(3)
    ow_third()
    ctx_ring.mid2(2)
    ctx_ring.mid2(3)
    for j in range(4):
        ctx_ring.fin(j)
    for j in range(8):
        if j == 2:
            ow_last()
        if j % 2 == 0:
            ow_ready(j // 2)
            out_units(j)
        out_ring.begin(j)
        if j >= 1:
            out_ring.mid1(j - 1)
        if j >= 2:
            out_ring.mid2(j - 2)
    for j in range(JOBS):
        proj.sent(j, 15)
    out_ring.mid1(7)
    out_ring.mid2(6)
    for q in range(QUARTERS):
        if q % 2 == 1:
            outw.sent(q, 15)
        else:
            @pl.when(c_is_hi)
            def _():
                outw.sent(q, 16)

            @pl.when(jnp.logical_not(c_is_hi))
            def _():
                outw.sent(q, 14)
    for j in range(4):
        ctx_ring.done(j)
    out_ring.mid2(7)
    for j in range(8):
        out_ring.fin(j)
    for j in range(8):
        out_ring.done(j)


def place_result(held, out, sem):
    flat = out.reshape(held.shape)
    copies = []
    for i in range(4):
        rows = pl.ds(i * 128, 128)
        copies.append(pltpu.make_async_copy(held.at[rows], flat.at[rows], sem.at[i]))
        copies[-1].start()
    for copy in copies:
        copy.wait()


def body(
    hidden_in, lengths, key_cache, value_cache, query_weight, key_weight, value_weight, out_weight
):
    row_count, step_count, width = hidden_in.shape
    slots = key_cache.shape[1]
    frequency = np.tile(rope_base ** (-(np.arange(HD // 2) * 2.0) / HD), 2).astype(np.float32)[None, :]
    hbm = pl.BlockSpec(memory_space=pl.ANY)
    vmem = pl.BlockSpec(memory_space=pltpu.VMEM)
    dma = pltpu.SemaphoreType.DMA
    result = pl.pallas_call(
        layer_kernel,
        out_shape=pltpu.VMEM((TOKENS, width), bf16),
        in_specs=[hbm] * 7 + [vmem] * 2,
        out_specs=vmem,
        scratch_shapes=[
            pltpu.VMEM((JOBS, width, LANES), bf16),
            pltpu.VMEM((QUARTERS, width, LANES), bf16),
            pltpu.VMEM((TOKENS, width), bf16),
            pltpu.VMEM((row_count * slots, HD), bf16),
            pltpu.VMEM((row_count * slots, HD), bf16),
            pltpu.VMEM((GROUP, TOKENS, HD), bf16),
            pltpu.VMEM((TOKENS, HD), bf16),
            pltpu.VMEM((TOKENS, HD), bf16),
            pltpu.VMEM((TP, 2, TOKENS, 2 * HD), bf16),
            pltpu.VMEM((TOKENS, 2 * LANES), f32),
            pltpu.VMEM((TOKENS, LANES), f32),
            pltpu.VMEM((TOKENS, LANES), f32),
            pltpu.VMEM((TOKENS, LANES), jnp.int32),
            dma((JOBS,)),
            dma((JOBS, 8)),
            dma((JOBS,)),
            dma((QUARTERS,)),
            dma((QUARTERS, 8)),
            dma((4,)),
            dma((4,)),
            dma((4, 8)),
            dma((8,)),
            dma((8, 8)),
            dma((3,)),
        ],
        compiler_params=pltpu.CompilerParams(
            collective_id=0, has_side_effects=True, vmem_limit_bytes=50 * 1024 * 1024
        ),
        name="attention_layer",
    )(
        hidden_in,
        key_cache.reshape(row_count * slots, HD),
        value_cache.reshape(row_count * slots, HD),
        query_weight, key_weight, value_weight, out_weight,
        lengths.reshape(1, row_count), jnp.asarray(frequency),
    )
    return pl.pallas_call(
        place_result,
        out_shape=jax.ShapeDtypeStruct(hidden_in.shape, bf16),
        in_specs=[vmem],
        out_specs=hbm,
        scratch_shapes=[dma((4,))],
        compiler_params=pltpu.CompilerParams(vmem_limit_bytes=1024 * 1024),
        name="place_result",
    )(result)


def solution(mesh):
    return jax.shard_map(
        body,
        mesh=mesh,
        in_specs=(
            P("fsdp", None, None),
            P("fsdp"),
            P("fsdp", None, "tp"),
            P("fsdp", None, "tp"),
            P("fsdp", None),
            P("fsdp", None),
            P("fsdp", None),
            P(None, "fsdp"),
        ),
        out_specs=P("fsdp", None, None),
        check_vma=False,
    )
```

time: 938 us -> 159 us (0.17)
  blocking collectives: 650 us -> 0 us
  Pallas kernels: 0 us -> 158 us
  waiting for transfers between devices: 111 us -> 0 us
  matrix products: 69.4 us -> 0 us
  local copies, waits for them, and re-layouts: 58 us -> 0 us
  other arithmetic: 29.5 us -> 0 us
  between operations: 13.8 us -> 0.01 us
    psum x1 -> x0, blocking collectives: 650 us -> none  [head_total(): return lax.psum(partial_blocks, 'tp').astype(jnp.bfloat16)]
    pallas_call x0 -> x2, Pallas kernels: none -> 158 us  [the longest x1 155 us: body(): pl.pallas_call(layer_kernel, out_shape=pltpu.VMEM((TOKENS, width), bf16),...]
    all_gather x4 -> x0, waiting for transfers between devices: 111 us -> none  [the longest x1 42.8 us: body(): lax.all_gather(out_rows, 'fsdp', axis=1, tiled=True)]
    dot_general x8 -> x0, matrix products: 69.4 us -> none  [the longest x1 19.5 us: body(): jnp.dot(normed, lax.all_gather(query_cols, 'fsdp', axis=0, tiled=True), p...]
    dot_general x2 -> x0, local copies, waits for them, and re-layouts: 23.9 us -> none  [the longest x1 12 us: body(): jnp.dot(context, lax.all_gather(out_rows, 'fsdp', axis=1, tiled=True), pr...]
    convert_element_type x3 -> x0, other arithmetic: 17.2 us -> none  [the longest x2 16.5 us: body(): normed = (flat_rows * lax.rsqrt(jnp.mean(flat_rows * flat_rows, axis=1, k...]
    another operation x1 -> x0, local copies, waits for them, and re-layouts: 14.5 us -> none  [body(): return result.reshape(row_count, step_count, model_width)]
    convert_element_type x1 -> x0, local copies, waits for them, and re-layouts: 11.4 us -> none  [head_total(): return lax.psum(partial_blocks, 'tp').astype(jnp.bfloat16)]
  transfers between devices with their start and end apart: 4 -> 0, of which waited for: 4 -> 0; matrix products, arithmetic and copies ran while one was open for 8% -> 0% of each run, Pallas kernels for 0% -> 0%
where the time goes in v2:
time: 159 us; the launch traced here: 158 us
  Pallas kernels  158 us (99%)
    pallas_call x1, Pallas kernels, body(): pl.pallas_call(layer_kernel, out_shape=pltpu.VMEM((TOKENS, width), bf16),...  155 us
    pallas_call x1, Pallas kernels, body(): pl.pallas_call(place_result, out_shape=jax.ShapeDtypeStruct(hidden_in.sha...  3.37 us

profile of v2, /device:TPU:0, one launch (start us, length us, event | category | flops | bytes accessed | tf_op | source)
XLA Modules:
  0.0 158.4 jit_solution(11832842754689001248)
XLA Ops:
  0.0 155.0 %attention_layer.1.held = bf16[512,8192]{1,0:T(8,128)(2,1)S(1)} custom-call(bf16[128,4,8192]{2,1,0:T(4,128)(2,1)} %hidden.1, bf16[16384,128]{1,0:T(8,128)(2,1)} %bitcast.3, bf16[16384,128]{1,0:T(8,128)(2,1)} %bitcast.4, bf16[512,4096]{1,0:T(8,128)(2,1)} %wq.1, bf16[512,1024]{1,0:T(8,128)(2,1)} %wk.1, bf16[512,1024]{1,0:T(8,128)(2,1)} %wv.1, ...), custom_call_target="tpu_custom_call" | custom-call | tf_op jit(solution)/shard_map/attention_layer/pallas_call | solution.py:518
  155.0 3.4 %place_result.1 = bf16[128,4,8192]{2,1,0:T(4,128)(2,1)} custom-call(bf16[512,8192]{1,0:T(8,128)(2,1)S(1)} %attention_layer.1.held), custom_call_target="tpu_custom_call" | custom-call | tf_op jit(solution)/shard_map/place_result/pallas_call | solution.py:560

commit v3 on v2

--- a/solution.py
+++ b/solution.py
@@ -27,6 +27,11 @@
 HALF = TOKENS // 2
 TP = 8
 UNITS = (0, 3, 1, 2, 4, 5, 6, 7)
+OUT_PAIRS = ((0, 0), (0, 2), (1, 0), (1, 2), (0, 4), (1, 4), (0, 6), (1, 6))
+OUT_ORDER = tuple((half, u + i) for half, u in OUT_PAIRS for i in range(2))
+OUT_JOBS = len(OUT_ORDER)
+CTX_ACROSS = (2, 2, 2, 2)
+OUT_ACROSS = (2, 2, 3) * 5 + (2,)
 
 
 def al(x, m):
@@ -108,20 +113,16 @@
     def source_of(j):
         return ((wk, LANES, 0), (wv, LANES, 0))[j] if j < 2 else (wq, GROUP * LANES, j - 2)
 
-    def first_a(j):
+    def cols_of(j, tt):
         source, width, head = source_of(j)
-        proj.load(j, source.at[:, pl.ds(al(t * width + head * LANES, LANES), LANES)], 0)
-
-    def first_x(j):
-        source, width, head = source_of(j)
-        cols = source.at[:, pl.ds(al((y * 2 + 1 - hi) * width + head * LANES, LANES), LANES)]
-        proj.put(j, cols, proj.held(j, 0), 3, d_cross)
-
-    def first_b(j):
-        proj.wait(j, 0)
-        proj.pass_on(j, 0, 2, d_zp)
-        proj.pass_on(j, 0, 1, d_zm)
-        proj.to_sib(j, 0)
+        return source.at[:, pl.ds(al(tt * width + head * LANES, LANES), LANES)]
+
+    def first(j):
+        own, dst = cols_of(j, t), proj.held(j, 0)
+        proj.put(j, own, dst, 2, d_zp)
+        proj.put(j, own, dst, 1, d_zm)
+        proj.put(j, cols_of(j, y * 2 + 1 - hi), dst, 3, d_cross)
+        proj.put(j, own, dst, 8, d_sib)
 
     def mid1(j):
         proj.wait(j, 1)
@@ -152,6 +153,7 @@
     def fin(j):
         proj.wait(j, 7)
         proj.to_sib(j, 7)
+        proj.wait(j, 0)
         proj.wait_sib(gsib.at[j])
 
     def ow_rows(q, half):
@@ -216,8 +218,8 @@
     peer = ((y, hi), (yp, hi), (ym, hi), (y, 1 - hi), (yp, 1 - hi), (ym, 1 - hi), (y2, hi), (y2, 1 - hi))
 
     class Ring:
-        def __init__(self, ssem, rsem, block, seven):
-            self.ssem, self.rsem, self.block, self.seven = ssem, rsem, block, seven
+        def __init__(self, ssem, rsem, block, seven, across):
+            self.ssem, self.rsem, self.block, self.seven, self.across = ssem, rsem, block, seven, across
 
         def at(self, j, kind):
             return self.block(j, peer[kind][0], peer[kind][1])
@@ -236,21 +238,34 @@
             self.forward(j, 0, 3, d_hi)
 
         def mid1(self, j):
+            up, three = j % 2 == 1, self.across[j] == 3
             self.wait(j, 1)
-            if j % 2 == 0:
+            if not up:
                 self.forward(j, 1, 6, d_ym)
+                if three:
+                    self.forward(j, 1, 4, d_hi)
             self.wait(j, 2)
-            if j % 2 == 1:
+            if up:
                 self.forward(j, 2, 6, d_yp)
+                if three:
+                    self.forward(j, 2, 5, d_hi)
             self.wait(j, 3)
-            self.forward(j, 3, 5, d_yp)
-            self.forward(j, 3, 4, d_ym)
+            if not (three and up):
+                self.forward(j, 3, 5, d_yp)
+            if not (three and not up):
+                self.forward(j, 3, 4, d_ym)
 
         def mid2(self, j):
+            up, one = j % 2 == 1, self.across[j] == 1
             self.wait(j, 6)
-            self.forward(j, 6, 7, d_hi)
+            if not one:
+                self.forward(j, 6, 7, d_hi)
             self.wait(j, 4)
+            if one and not up:
+                self.forward(j, 4, 7, d_ym)
             self.wait(j, 5)
+            if one and up:
+                self.forward(j, 5, 7, d_yp)
 
         def fin(self, j):
             self.wait(j, 7)
@@ -261,15 +276,16 @@
     def ctx_block(j, yy, hh):
         return ctx.at[yy * 2 + hh, j // 2, pl.ds((j % 2) * HALF, HALF)]
 
-    def out_cols(j, yy, hh):
-        zz, ll = place[UNITS[j]]
+    def out_cols(u, yy, hh):
+        zz, ll = place[UNITS[u]]
         return pl.ds(al(((zz * 2 + ll) * 2 + hh) * BLOCK + yy * LANES, LANES), LANES)
 
     def out_block(j, yy, hh):
-        return out.at[:, out_cols(j, yy, hh)]
-
-    ctx_ring = Ring(csend, crecv, ctx_block, ctx.at[pl.ds(0, 7), 0, pl.ds(0, HALF)])
-    out_ring = Ring(osend, orecv, out_block, out.at[:, pl.ds(0, 7 * LANES)])
+        half, u = OUT_ORDER[j]
+        return out.at[pl.ds(half * HALF, HALF), out_cols(u, yy, hh)]
+
+    ctx_ring = Ring(csend, crecv, ctx_block, ctx.at[pl.ds(0, 7), 0, pl.ds(0, HALF)], CTX_ACROSS)
+    out_ring = Ring(osend, orecv, out_block, out.at[pl.ds(0, HALF), pl.ds(0, 7 * LANES)], OUT_ACROSS)
 
     def tables():
         def part(i, _):
@@ -372,24 +388,26 @@
             tok = slice(i * 128 + b * 16, i * 128 + (b + 1) * 16)
             ctx[t, p, tok, :] = jnp.concatenate([mixes[b][:16], mixes[b][16:]], axis=1)
 
-    def out_units(j):
-        acc[...] = jnp.zeros_like(acc)
-        slots = [(place[UNITS[j + i]][0] * 2 + place[UNITS[j + i]][1]) * 2 for i in range(2)]
+    def out_units(half, u):
+        rows = slice(half * HALF, (half + 1) * HALF)
+        part_sum = acc.at[:HALF]
+        part_sum[...] = jnp.zeros_like(part_sum)
+        slots = [(place[UNITS[u + i]][0] * 2 + place[UNITS[u + i]][1]) * 2 for i in range(2)]
 
         def part(i, _):
             def weights(tt):
-                half = tt // 4
-                pieces = [wobuf[tt % 4, pl.ds(al((slot + half) * BLOCK, BLOCK), BLOCK), :] for slot in slots]
+                side = tt // 4
+                pieces = [wobuf[tt % 4, pl.ds(al((slot + side) * BLOCK, BLOCK), BLOCK), :] for slot in slots]
                 return jnp.concatenate(pieces, axis=1)
 
-            left = jnp.concatenate([ctx[2 * i, 0], ctx[2 * i, 1], ctx[2 * i + 1, 0], ctx[2 * i + 1, 1]], axis=1)
+            left = jnp.concatenate([ctx[2 * i + k // 2, k % 2, rows, :] for k in range(4)], axis=1)
             right = jnp.concatenate([weights(2 * i), weights(2 * i + 1)], axis=0)
-            acc[...] += jnp.dot(left, right, preferred_element_type=f32)
+            part_sum[...] += jnp.dot(left, right, preferred_element_type=f32)
             return 0
 
         lax.fori_loop(0, TP // 2, part, 0)
         for i in range(2):
-            out[:, out_cols(j + i, y, hi)] = acc[:, i * LANES:(i + 1) * LANES].astype(bf16)
+            out[rows, out_cols(u + i, y, hi)] = part_sum[:, i * LANES:(i + 1) * LANES].astype(bf16)
 
     xload = pltpu.make_async_copy(hidden.reshape(TOKENS, hidden.shape[2]), xn, local_sem.at[0])
     kload = pltpu.make_async_copy(kcache, kc, local_sem.at[1])
@@ -398,24 +416,20 @@
     partners = (d_hi, d_zp, d_zm, d_yp, d_ym, d_pair, d_cross, d_cross_sib, d_sib)
     for device in partners:
         pl.semaphore_signal(barrier, inc=1, device_id=device, device_id_type=MESH)
-    for j in range(3):
-        first_a(j)
+    for j in range(JOBS):
+        proj.load(j, cols_of(j, t), 0)
     xload.start()
     kload.start()
     vload.start()
     tables()
     pl.semaphore_wait(barrier, len(partners))
-    for j in range(2):
-        first_x(j)
-        first_b(j)
+    first(0)
+    first(1)
     xload.wait()
     lax.fori_loop(0, TOKENS // 64, norm, 0)
     for j in range(4):
         mid1(j)
-        first_x(j + 2)
-        first_b(j + 2)
-        if j < 3:
-            first_a(j + 3)
+        first(j + 2)
         if j >= 1:
             mid2(j - 1)
         if j >= 2:
@@ -432,7 +446,6 @@
     kload.wait()
     vload.wait()
     mid2(5)
-    ow_first()
     attend(0, 0)
     attend(0, 1)
     ctx_ring.begin(0)
@@ -440,41 +453,47 @@
     attend(0, 2)
     attend(0, 3)
     ctx_ring.begin(1)
+    ctx_ring.mid1(0)
     fin(5)
+    ow_first()
+    ctx_ring.mid1(1)
     project(2)
-    ctx_ring.mid1(0)
+    ctx_ring.mid2(0)
     attend(1, 0)
     attend(1, 1)
     ctx_ring.begin(2)
-    ctx_ring.mid1(1)
+    ctx_ring.mid2(1)
     attend(1, 2)
     attend(1, 3)
     ctx_ring.begin(3)
+    ctx_ring.mid1(2)
     ow_second()
-    ctx_ring.mid2(0)
-    ctx_ring.mid1(2)
-    ctx_ring.mid2(1)
     ctx_ring.mid1(3)
-    ow_third()
     ctx_ring.mid2(2)
+    ctx_ring.fin(0)
+    ctx_ring.fin(2)
     ctx_ring.mid2(3)
-    for j in range(4):
-        ctx_ring.fin(j)
-    for j in range(8):
-        if j == 2:
+    for j in range(OUT_JOBS):
+        if j == 4:
+            ctx_ring.fin(1)
+            ctx_ring.fin(3)
+            ow_third()
+        if j == 8:
             ow_last()
         if j % 2 == 0:
-            ow_ready(j // 2)
-            out_units(j)
+            half, u = OUT_ORDER[j]
+            if half == 0:
+                ow_ready(u // 2)
+            out_units(half, u)
         out_ring.begin(j)
-        if j >= 1:
-            out_ring.mid1(j - 1)
         if j >= 2:
-            out_ring.mid2(j - 2)
+            out_ring.mid1(j - 2)
+        if j >= 4:
+            out_ring.mid2(j - 4)
     for j in range(JOBS):
         proj.sent(j, 15)
-    out_ring.mid1(7)
-    out_ring.mid2(6)
+    out_ring.mid2(OUT_JOBS - 4)
+    out_ring.mid1(OUT_JOBS - 2)
     for q in range(QUARTERS):
         if q % 2 == 1:
             outw.sent(q, 15)
@@ -486,12 +505,15 @@
             @pl.when(jnp.logical_not(c_is_hi))
             def _():
                 outw.sent(q, 14)
+    out_ring.mid2(OUT_JOBS - 3)
+    out_ring.mid1(OUT_JOBS - 1)
     for j in range(4):
         ctx_ring.done(j)
-    out_ring.mid2(7)
-    for j in range(8):
+    out_ring.mid2(OUT_JOBS - 2)
+    out_ring.mid2(OUT_JOBS - 1)
+    for j in range(OUT_JOBS):
         out_ring.fin(j)
-    for j in range(8):
+    for j in range(OUT_JOBS):
         out_ring.done(j)
 
 
@@ -542,8 +564,8 @@
             dma((4,)),
             dma((4,)),
             dma((4, 8)),
-            dma((8,)),
-            dma((8, 8)),
+            dma((OUT_JOBS,)),
+            dma((OUT_JOBS, 8)),
             dma((3,)),
         ],
         compiler_params=pltpu.CompilerParams(

time: 159 us -> 151 us (0.950)
  Pallas kernels: 158 us -> 151 us
    pallas_call x1, Pallas kernels: 155 us -> 147 us  [body(): pl.pallas_call(layer_kernel, out_shape=pltpu.VMEM((TOKENS, width), bf16),...]
where the time goes in v3:
time: 151 us
  Pallas kernels  151 us (100%)
    pallas_call x1, Pallas kernels, body(): pl.pallas_call(layer_kernel, out_shape=pltpu.VMEM((TOKENS, width), bf16),...  147 us
    pallas_call x1, Pallas kernels, body(): pl.pallas_call(place_result, out_shape=jax.ShapeDtypeStruct(hidden_in.sha...  3.37 us

profile of v3, /device:TPU:0, one launch (start us, length us, event | category | flops | bytes accessed | tf_op | source)
XLA Modules:
  0.0 150.6 jit_solution(9648252997811154399)
XLA Ops:
  0.0 147.3 %attention_layer.1.held = bf16[512,8192]{1,0:T(8,128)(2,1)S(1)} custom-call(bf16[128,4,8192]{2,1,0:T(4,128)(2,1)} %hidden.1, bf16[16384,128]{1,0:T(8,128)(2,1)} %bitcast.3, bf16[16384,128]{1,0:T(8,128)(2,1)} %bitcast.4, bf16[512,4096]{1,0:T(8,128)(2,1)} %wq.1, bf16[512,1024]{1,0:T(8,128)(2,1)} %wk.1, bf16[512,1024]{1,0:T(8,128)(2,1)} %wv.1, ...), custom_call_target="tpu_custom_call" | custom-call | tf_op jit(solution)/shard_map/attention_layer/pallas_call | solution.py:540
  147.3 3.4 %place_result.1 = bf16[128,4,8192]{2,1,0:T(4,128)(2,1)} custom-call(bf16[512,8192]{1,0:T(8,128)(2,1)S(1)} %attention_layer.1.held), custom_call_target="tpu_custom_call" | custom-call | tf_op jit(solution)/shard_map/place_result/pallas_call | solution.py:582

commit v4 on v3

--- a/solution.py
+++ b/solution.py
@@ -30,7 +30,8 @@
 OUT_PAIRS = ((0, 0), (0, 2), (1, 0), (1, 2), (0, 4), (1, 4), (0, 6), (1, 6))
 OUT_ORDER = tuple((half, u + i) for half, u in OUT_PAIRS for i in range(2))
 OUT_JOBS = len(OUT_ORDER)
-CTX_ACROSS = (2, 2, 2, 2)
+CTX_JOBS = 2 * GROUP
+CTX_ACROSS = (2,) * CTX_JOBS
 OUT_ACROSS = (2, 2, 3) * 5 + (2,)
 
 
@@ -323,38 +324,39 @@
         lax.fori_loop(0, width // 512, apply, 0)
         return 0
 
-    def project(p):
-        acc[...] = jnp.zeros_like(acc)
+    def rotated(v):
+        return (v * cos_ref[...] + pltpu.roll(v, HD // 2, 1) * sin_ref[...]).astype(bf16)
+
+    def product(total, depth, weights):
+        total[...] = jnp.zeros_like(total)
 
         def part(k, _):
-            cols = pl.ds(al(k * 1024, 1024), 1024)
-            weights = jnp.concatenate([wbuf[2 * p, cols, :], wbuf[2 * p + 1, cols, :]], axis=1)
-            acc[...] += jnp.dot(xn[:, cols], weights, preferred_element_type=f32)
+            rows = pl.ds(al(k * depth, depth), depth)
+            total[...] += jnp.dot(xn[:, rows], weights(rows), preferred_element_type=f32)
             return 0
 
-        lax.fori_loop(0, 8, part, 0)
-
-        def rotated(v):
-            return (v * cos_ref[...] + pltpu.roll(v, HD // 2, 1) * sin_ref[...]).astype(bf16)
-
-        if p == 0:
-            kn[...] = rotated(acc[:, :HD])
-            vn[...] = acc[:, HD:].astype(bf16)
-        else:
-            qr[2 * p - 2] = rotated(acc[:, :HD])
-            qr[2 * p - 1] = rotated(acc[:, HD:])
+        lax.fori_loop(0, xn.shape[1] // depth, part, 0)
+
+    def project_kv():
+        product(acc, 1024, lambda rows: jnp.concatenate([wbuf[0, rows, :], wbuf[1, rows, :]], axis=1))
+        kn[...] = rotated(acc[:, :HD])
+        vn[...] = acc[:, HD:].astype(bf16)
+
+    def project_q(h):
+        product(acc.at[:, :HD], 2048, lambda rows: wbuf[2 + h, rows, :])
+        qr[h] = rotated(acc[:, :HD])
 
     scaling = 1.0 / math.sqrt(HD)
     nt = (((1,), (1,)), ((), ()))
 
-    def attend(p, i):
+    def attend(h, i):
         fresh = slice(i * 128, (i + 1) * 128)
-        token = lax.broadcasted_iota(jnp.int32, (32, 1), 0) % 16
+        token = lax.broadcasted_iota(jnp.int32, (16, 1), 0)
         row = token // STEPS
         scores = []
         for b in range(8):
             tok = slice(i * 128 + b * 16, i * 128 + (b + 1) * 16)
-            q = jnp.concatenate([qr[2 * p, tok, :], qr[2 * p + 1, tok, :]], axis=0)
+            q = qr[h, tok, :]
             keys = kc[(i * 8 + b) * 512:(i * 8 + b + 1) * 512, :]
             older = lax.dot_general(q, keys, nt, preferred_element_type=f32) * scaling
             recent = lax.dot_general(q, kn[fresh, :], nt, preferred_element_type=f32) * scaling
@@ -362,17 +364,16 @@
         for b in range(8):
             older, recent = scores[b]
             live = len_ref[i * 128 + b * 16:i * 128 + (b + 1) * 16, :1]
-            live = jnp.concatenate([live, live], axis=0)
             lane = lax.broadcasted_iota(jnp.int32, older.shape, 1)
             older = jnp.where((lane >= row * 128) & (lane < row * 128 + live), older, masked)
             lane = lax.broadcasted_iota(jnp.int32, recent.shape, 1) - b * 16
             recent = jnp.where((lane >= row * STEPS) & (lane <= token), recent, masked)
             scores[b] = older, recent
-        highest = [
+        tops = [
             jnp.maximum(jnp.max(older, axis=1, keepdims=True), jnp.max(recent, axis=1, keepdims=True))
             for older, recent in scores
         ]
-        scores = [(jnp.exp(older - h), jnp.exp(recent - h)) for (older, recent), h in zip(scores, highest)]
+        scores = [(jnp.exp(older - h), jnp.exp(recent - h)) for (older, recent), h in zip(scores, tops)]
         inverse = [
             1.0 / (jnp.sum(older, axis=1, keepdims=True) + jnp.sum(recent, axis=1, keepdims=True))
             for older, recent in scores
@@ -386,7 +387,7 @@
             mixes.append(mix.astype(bf16))
         for b in range(8):
             tok = slice(i * 128 + b * 16, i * 128 + (b + 1) * 16)
-            ctx[t, p, tok, :] = jnp.concatenate([mixes[b][:16], mixes[b][16:]], axis=1)
+            ctx[t, h, tok, :] = mixes[b]
 
     def out_units(half, u):
         rows = slice(half * HALF, (half + 1) * HALF)
@@ -400,7 +401,7 @@
                 pieces = [wobuf[tt % 4, pl.ds(al((slot + side) * BLOCK, BLOCK), BLOCK), :] for slot in slots]
                 return jnp.concatenate(pieces, axis=1)
 
-            left = jnp.concatenate([ctx[2 * i + k // 2, k % 2, rows, :] for k in range(4)], axis=1)
+            left = jnp.concatenate([ctx[2 * i + k // 4, k % 4, rows, :] for k in range(8)], axis=1)
             right = jnp.concatenate([weights(2 * i), weights(2 * i + 1)], axis=0)
             part_sum[...] += jnp.dot(left, right, preferred_element_type=f32)
             return 0
@@ -434,49 +435,73 @@
             mid2(j - 1)
         if j >= 2:
             fin(j - 2)
-    project(0)
+    project_kv()
     mid1(4)
     mid2(3)
     fin(2)
     ow_load()
-    mid1(5)
-    mid2(4)
-    fin(3)
-    project(1)
+    project_q(0)
     kload.wait()
     vload.wait()
-    mid2(5)
+    mid1(5)
     attend(0, 0)
     attend(0, 1)
     ctx_ring.begin(0)
-    fin(4)
+    mid2(4)
+    fin(3)
     attend(0, 2)
     attend(0, 3)
     ctx_ring.begin(1)
+    project_q(1)
+    mid2(5)
+    fin(4)
     ctx_ring.mid1(0)
-    fin(5)
-    ow_first()
-    ctx_ring.mid1(1)
-    project(2)
-    ctx_ring.mid2(0)
     attend(1, 0)
     attend(1, 1)
     ctx_ring.begin(2)
-    ctx_ring.mid2(1)
+    ctx_ring.mid1(1)
     attend(1, 2)
     attend(1, 3)
     ctx_ring.begin(3)
+    ctx_ring.mid2(0)
+    fin(5)
+    ow_first()
+    project_q(2)
     ctx_ring.mid1(2)
+    attend(2, 0)
+    attend(2, 1)
+    ctx_ring.begin(4)
+    ctx_ring.mid1(3)
+    ctx_ring.mid2(1)
+    attend(2, 2)
+    attend(2, 3)
+    ctx_ring.begin(5)
+    project_q(3)
+    ctx_ring.mid1(4)
+    ctx_ring.mid2(2)
+    attend(3, 0)
+    attend(3, 1)
+    ctx_ring.begin(6)
+    ctx_ring.mid1(5)
+    ctx_ring.mid2(3)
+    attend(3, 2)
+    attend(3, 3)
+    ctx_ring.begin(7)
+    ctx_ring.mid2(4)
+    ctx_ring.mid1(6)
+    ctx_ring.mid2(5)
+    ctx_ring.mid1(7)
     ow_second()
-    ctx_ring.mid1(3)
-    ctx_ring.mid2(2)
+    ctx_ring.mid2(6)
     ctx_ring.fin(0)
     ctx_ring.fin(2)
-    ctx_ring.mid2(3)
+    ctx_ring.fin(4)
+    ctx_ring.fin(6)
+    ctx_ring.mid2(7)
     for j in range(OUT_JOBS):
         if j == 4:
-            ctx_ring.fin(1)
-            ctx_ring.fin(3)
+            for k in range(1, CTX_JOBS, 2):
+                ctx_ring.fin(k)
             ow_third()
         if j == 8:
             ow_last()
@@ -507,7 +532,7 @@
                 outw.sent(q, 14)
     out_ring.mid2(OUT_JOBS - 3)
     out_ring.mid1(OUT_JOBS - 1)
-    for j in range(4):
+    for j in range(CTX_JOBS):
         ctx_ring.done(j)
     out_ring.mid2(OUT_JOBS - 2)
     out_ring.mid2(OUT_JOBS - 1)
@@ -551,7 +576,7 @@
             pltpu.VMEM((GROUP, TOKENS, HD), bf16),
             pltpu.VMEM((TOKENS, HD), bf16),
             pltpu.VMEM((TOKENS, HD), bf16),
-            pltpu.VMEM((TP, 2, TOKENS, 2 * HD), bf16),
+            pltpu.VMEM((TP, GROUP, TOKENS, HD), bf16),
             pltpu.VMEM((TOKENS, 2 * LANES), f32),
             pltpu.VMEM((TOKENS, LANES), f32),
             pltpu.VMEM((TOKENS, LANES), f32),
@@ -562,8 +587,8 @@
             dma((QUARTERS,)),
             dma((QUARTERS, 8)),
             dma((4,)),
-            dma((4,)),
-            dma((4, 8)),
+            dma((CTX_JOBS,)),
+            dma((CTX_JOBS, 8)),
             dma((OUT_JOBS,)),
             dma((OUT_JOBS, 8)),
             dma((3,)),

time: 151 us -> 151 us (level)
  no operation moved by 1% of the time
where the time goes in v4:
time: 151 us
  Pallas kernels  151 us (100%)
    pallas_call x1, Pallas kernels, body(): pl.pallas_call(layer_kernel, out_shape=pltpu.VMEM((TOKENS, width), bf16),...  148 us
    pallas_call x1, Pallas kernels, body(): pl.pallas_call(place_result, out_shape=jax.ShapeDtypeStruct(hidden_in.sha...  3.37 us

profile of v4, /device:TPU:0, one launch (start us, length us, event | category | flops | bytes accessed | tf_op | source)
XLA Modules:
  0.0 151.2 jit_solution(13654501274752243660)
XLA Ops:
  0.0 147.7 %attention_layer.1.held = bf16[512,8192]{1,0:T(8,128)(2,1)S(1)} custom-call(bf16[128,4,8192]{2,1,0:T(4,128)(2,1)} %hidden.1, bf16[16384,128]{1,0:T(8,128)(2,1)} %bitcast.3, bf16[16384,128]{1,0:T(8,128)(2,1)} %bitcast.4, bf16[512,4096]{1,0:T(8,128)(2,1)} %wq.1, bf16[512,1024]{1,0:T(8,128)(2,1)} %wk.1, bf16[512,1024]{1,0:T(8,128)(2,1)} %wv.1, ...), custom_call_target="tpu_custom_call" | custom-call | tf_op jit(solution)/shard_map/attention_layer/pallas_call | solution.py:565
  147.7 3.4 %place_result.1 = bf16[128,4,8192]{2,1,0:T(4,128)(2,1)} custom-call(bf16[512,8192]{1,0:T(8,128)(2,1)S(1)} %attention_layer.1.held), custom_call_target="tpu_custom_call" | custom-call | tf_op jit(solution)/shard_map/place_result/pallas_call | solution.py:607
